TPU v7x, 32 devices: a whole 2x2x4 slice. The times are simulated.
32 devices in a mesh: groups: 2 (over y), src: 4 (over z), tgt: 2 (over x), dir: 2 (over core).
Axes of the slice: x: 2, y: 2, z: 4, core: 2. Of those that a mesh axis runs over, the one named last changes fastest.
Arguments:
- incident: bfloat16 [2, 64, 4096], P(None, 'dir', ('groups', 'src')), parts along dimension 2, may hold values from -6 to 6
- near_blocks: bfloat16 [8, 2, 56, 2, 128, 128], P(('groups', 'src'), 'tgt'), parts along dimension 0, may hold values from -0.25 to 0.25
- near_src: int32 [8, 2, 56], P(('groups', 'src'), 'tgt'), parts along dimension 0, may hold values from 0 to 3
- near_tgt: int32 [8, 2, 56], P(('groups', 'src'), 'tgt'), parts along dimension 0, may hold values from 0 to 15, as said below
- far_v: bfloat16 [8, 2, 32, 2, 32, 128], P(('groups', 'src'), 'tgt'), parts along dimension 0, may hold values from -0.5 to 0.5
- far_src: int32 [8, 2, 32], P(('groups', 'src'), 'tgt'), parts along dimension 0, may hold values from 0 to 3
- far_dst: int32 [8, 2, 32], P(('groups', 'src'), 'tgt'), parts along dimension 0, may hold values from 0 to 127, as said below
- far_u: bfloat16 [8, 2, 32, 2, 32, 128], P(('groups', 'src'), 'tgt'), parts along dimension 0, may hold values from -0.75 to 0.75
- far_tgt: int32 [8, 2, 32], P(('groups', 'src'), 'tgt'), parts along dimension 0, may hold values from 0 to 3
Outputs:
- potential: float32 [2, 64, 4096], P(None, 'dir', ('groups', 'src', 'tgt')), parts along dimension 2
There are 2 independent parts, one for each index of `groups`. A program takes and returns all parts, laid end to end along the dimension named above; each array names one. Nothing has to cross between parts.
Inputs may be any that keep to these rules, and one draw needn't show every extreme that they name: Near block (s, t, b) aims at owner near_tgt // 4. The near blocks of one device aimed at one owner other than s number at most 2 and reach at most 1 distinct target cluster; in every draw some owner receives exactly 2 near blocks from every device of every other owner. `far_dst`: value v names owner v // 32 and slot v % 32 at the same tgt index. Among the devices of one tgt index every value occurs exactly once; one device sends exactly 8 far blocks or none to each owner.
All inputs are finite; a program needn't handle non-finite values.
Results may differ from a plain program's by a relative error of at most 0.0025.
Values may be sent and summed in bfloat16 or wider, within the bound.
A program may use at most 64 MiB of HBM per device.

v0:
```python
import jax
import jax.numpy as jnp
from jax import lax
from jax.sharding import PartitionSpec as P

PANEL = 128
CAP = 2


def complex_apply(operand, matrices, pattern):
    products = jnp.einsum(pattern, operand, matrices, preferred_element_type=jnp.float32)
    return jnp.stack(
        [products[:, 0, 0] - products[:, 1, 1], products[:, 1, 0] + products[:, 0, 1]], axis=1
    )


def place_rows(targets, owners, slot_depth):
    position = jnp.arange(targets.shape[0], dtype=jnp.int32)
    earlier = (targets[:, None] == targets[None, :]) & (position[:, None] < position[None, :])
    rank_in = jnp.sum(earlier.astype(jnp.int32), axis=0)
    slot_of = jnp.where(targets >= 0, targets * slot_depth + rank_in, -1)
    slot_hits = slot_of[None, :] == jnp.arange(owners * slot_depth, dtype=jnp.int32)[:, None]
    chosen = jnp.sum(slot_hits.astype(jnp.int32) * position[None, :], axis=1)
    return (chosen, jnp.any(slot_hits, axis=1))


def cluster_sum(labels, values, clusters):
    one_hot = (labels[None, :] == jnp.arange(clusters, dtype=jnp.int32)[:, None]).astype(
        jnp.float32
    )
    return jnp.einsum("lr,radp->adlp", one_hot, values, precision=lax.Precision.HIGHEST)


def body(incident, near_blocks, near_src, near_tgt, far_v, far_src, far_dst, far_u, far_tgt):
    owners = lax.axis_size("src")
    my_owner = lax.axis_index("src")
    half_dirs = incident.shape[1]
    own_clusters = incident.shape[2] // PANEL
    source = incident.reshape(2, half_dirs, own_clusters, PANEL)
    blocks = near_blocks.reshape((-1,) + near_blocks.shape[3:])
    near_from = near_src.reshape(-1)
    near_to = near_tgt.reshape(-1)
    picked = jnp.take(source, near_from, axis=2)
    partial_value = complex_apply(picked, blocks, "adbq,bcpq->bacdp")
    dest_owner = near_to // own_clusters
    local_cluster = near_to % own_clusters
    is_mine = dest_owner == my_owner
    remote = jnp.where(is_mine, -1, dest_owner)
    own_sum = cluster_sum(jnp.where(is_mine, local_cluster, -1), partial_value, own_clusters)
    chosen, filled = place_rows(remote, owners, CAP)
    outgoing = jnp.where(filled[:, None, None, None], partial_value[chosen], 0.0)
    labels = jnp.where(filled, local_cluster[chosen], -1)
    arrived, arrived_labels = (
        lax.all_to_all(
            outgoing.reshape(owners, CAP, 2, half_dirs, PANEL),
            "src",
            split_axis=0,
            concat_axis=0,
            tiled=True,
        ),
        lax.all_to_all(labels.reshape(owners, CAP), "src", split_axis=0, concat_axis=0, tiled=True),
    )
    arrived_rows = arrived.reshape((-1, 2, half_dirs, PANEL))
    near_in = cluster_sum(arrived_labels.reshape(-1), arrived_rows, own_clusters)
    far_count = far_v.shape[2]
    far_from = far_src.reshape(-1)
    far_factors = far_v.reshape((-1,) + far_v.shape[3:])
    coefficients = complex_apply(
        jnp.take(source, far_from, axis=2), far_factors, "adbq,bckq->bacdk"
    ).astype(jnp.bfloat16)
    routed = far_dst.reshape(-1)
    slot_depth = max(2, far_count // owners)
    chosen_far, filled_far = place_rows(routed // far_count, owners, slot_depth)
    outgoing_far = jnp.where(filled_far[:, None, None, None], coefficients[chosen_far], 0)
    slot_far = jnp.where(filled_far, routed[chosen_far] % far_count, -1)
    received, received_slot = (
        lax.all_to_all(
            outgoing_far.reshape((owners, slot_depth) + coefficients.shape[1:]),
            "src",
            split_axis=0,
            concat_axis=0,
            tiled=True,
        ),
        lax.all_to_all(
            slot_far.reshape(owners, slot_depth), "src", split_axis=0, concat_axis=0, tiled=True
        ),
    )
    received_slot = received_slot.reshape(-1)
    slot_match = received_slot[None, :] == jnp.arange(far_count, dtype=jnp.int32)[:, None]
    row_index = jnp.sum(
        slot_match.astype(jnp.int32) * jnp.arange(received_slot.shape[0], dtype=jnp.int32)[None, :],
        axis=1,
    )
    matched = jnp.take(received.reshape((-1,) + coefficients.shape[1:]), row_index, axis=0)
    potential = complex_apply(matched, far_u.reshape((-1,) + far_u.shape[3:]), "badk,bckp->bacdp")
    far_in = cluster_sum(far_tgt.reshape(-1), potential, own_clusters)
    cluster_total = own_sum + near_in + far_in
    result = lax.psum_scatter(cluster_total, "tgt", scatter_dimension=2, tiled=True)
    return result.reshape(2, half_dirs, -1)


def solution(mesh):
    placed = (
        P(None, "dir", ("groups", "src")),
        P(("groups", "src"), "tgt", None, None, None, None),
        P(("groups", "src"), "tgt", None),
        P(("groups", "src"), "tgt", None),
        P(("groups", "src"), "tgt", None, None, None, None),
        P(("groups", "src"), "tgt", None),
        P(("groups", "src"), "tgt", None),
        P(("groups", "src"), "tgt", None, None, None, None),
        P(("groups", "src"), "tgt", None),
    )
    return jax.shard_map(
        body,
        mesh=mesh,
        in_specs=placed,
        out_specs=P(None, "dir", ("groups", "src", "tgt")),
        check_vma=False,
    )
```

profile of v0, /device:TPU:0, one launch (start us, length us, event | category | flops | bytes accessed | tf_op | source)
XLA Modules:
  0.0 88.7 jit_solution(1472638785312227239)
XLA Ops:
  6.5 0.7 compare_select_fusion.9
  8.9 6.3 %all-to-all-start.1 = ((s32[4,1,2]{2,1,0:T(1,128)}), s32[4,1,2]{2,1,0:T(1,128)S(1)}, u32[]{:S(2)}, u32[]{:S(2)}) async-start(s32[4,1,2]{2,1,0:T(1,128)} %bitcast.19), calls=%async_computation.1 | async-start | bytes 4096 | tf_op jit(solution)/shard_map/all_to_all | solution.py:61
  16.6 0.8 copy_bitcast_fusion.1
  18.2 3.5 %fusion.2 = f32[56,2,2,32,128]{4,3,2,1,0:T(8,128)S(1)} fusion(bf16[1,1,56,2,128,128]{5,4,3,2,1,0:T(8,128)(2,1)} %param.10, bf16[56,2,32,128]{3,2,1,0:T(8,128)(2,1)S(1)} %gather_fusion, pred[56]{0:T(512)(128)(4,1)S(1)} %compare_and_fusion.2), kind=kOutput, calls=%fused_computation.9 | convolution fusion | flops 235339776 | bytes 8257592 | tf_op jit(solution)/shard_map/adbq,bcpq->bacdp/dot_general | solution.py:11
  21.9 1.1 %fusion.20 = f32[56,1,32,128]{3,2,0,1:T(8,128)} fusion(f32[56,2,2,32,128]{4,3,2,1,0:T(8,128)S(1)} %fusion.2), kind=kLoop, calls=%fused_computation.25 | loop fusion | flops 229376 | bytes 2752512 | tf_op jit(solution)/shard_map/sub | solution.py:13
  23.7 1.0 %convolution_bitcast_fusion.1 = f32[32,2,2,32,32]{4,3,2,1,0:T(8,128)S(1)} fusion(bf16[1,1,32,2,32,128]{5,4,3,2,1,0:T(8,128)(2,1)S(1)} %copy-done.2, bf16[32,2,32,128]{3,2,1,0:T(8,128)(2,1)S(1)} %gather_fusion.4, pred[32]{0:T(512)(128)(4,1)S(1)} %compare_and_fusion), kind=kOutput, calls=%fused_computation.14 | convolution fusion | flops 33816576 | bytes 1572896 | tf_op jit(solution)/shard_map/adbq,bckq->bacdk/dot_general | solution.py:11
  24.8 0.8 fusion.39
  25.6 0.8 fusion.40
  26.9 1.4 %pad_maximum_fusion = f32[56,2,32,128]{3,2,0,1:T(8,128)S(1)} fusion(f32[56,1,32,128]{3,2,0,1:T(8,128)S(1)} %fusion.18, f32[56,1,32,128]{3,2,0,1:T(8,128)} %fusion.20), kind=kLoop, calls=%fused_computation.10 | loop fusion | flops 458752 | bytes 3670016 | tf_op jit(solution)/shard_map/stack | solution.py:12
  28.2 1.3 %gather_fusion.1 = f32[8,2,32,128]{3,2,1,0:T(8,128)} fusion(f32[56,2,32,128]{3,2,0,1:T(8,128)S(1)} %pad_maximum_fusion, s32[1024]{0:T(1024)S(1)} %pad_clamp_fusion.3), kind=kCustom, calls=%fused_computation.1 | custom fusion | bytes 524320 | tf_op jit(solution)/shard_map/gather | solution.py:51
  29.5 1.1 %pad_maximum_fusion.2 = bf16[32,2,32,32]{3,2,0,1:T(8,128)(2,1)S(1)} fusion(bf16[32,1,32,32]{3,2,0,1:T(8,128)(2,1)} %fusion.40, bf16[32,1,32,32]{3,2,0,1:T(8,128)(2,1)} %fusion.39), kind=kLoop, calls=%fused_computation.42 | loop fusion | flops 65536 | bytes 262144 | tf_op jit(solution)/shard_map/stack | solution.py:12
  31.4 1.2 %reshape.635 = bf16[4,2,8192]{2,1,0:T(2,128)(2,1)} reshape(bf16[4,8,2,32,32]{4,3,2,1,0:T(8,128)(2,1)S(1)} %broadcast_select_fusion) | data formatting | bytes 262144
  33.4 1.7 %broadcast_select_fusion.1 = f32[4,2,2,32,128]{4,3,2,1,0:T(8,128)} fusion(f32[4,2,2,32,128]{4,3,2,1,0:T(8,128)} %bitcast.177, pred[4,2]{1,0:T(4,128)(4,1)S(1)} %broadcast_in_dim.100), kind=kLoop, calls=%fused_computation.57 | loop fusion | flops 65536 | bytes 524296 | tf_op jit(solution)/shard_map/jit(_where)/select_n | solution.py:51
  35.7 5.1 %all-to-all-start.2 = ((s32[4,1,8]{2,1,0:T(1,128)}), s32[4,1,8]{2,1,0:T(1,128)S(1)}, u32[]{:S(2)}, u32[]{:S(2)}) async-start(s32[4,1,8]{2,1,0:T(1,128)} %bitcast.25), calls=%async_computation.2 | async-start | bytes 4096 | tf_op jit(solution)/shard_map/all_to_all | solution.py:84
  42.1 4.2 %all-to-all-done.2 = s32[4,1,8]{2,1,0:T(1,128)S(1)} async-done(((s32[4,1,8]{2,1,0:T(1,128)}), s32[4,1,8]{2,1,0:T(1,128)S(1)}, u32[]{:S(2)}, u32[]{:S(2)}) %all-to-all-start.2) | async-done | bytes 160 | tf_op jit(solution)/shard_map/all_to_all | solution.py:84
  46.3 3.3 %all-to-all-start.3 = ((bf16[4,2,8192]{2,1,0:T(2,128)(2,1)}), bf16[4,2,8192]{2,1,0:T(2,128)(2,1)S(1)}, u32[]{:S(2)}, u32[]{:S(2)}) async-start(bf16[4,2,8192]{2,1,0:T(2,128)(2,1)} %reshape.635), calls=%async_computation.3 | async-start | bytes 262144 | tf_op jit(solution)/shard_map/all_to_all | solution.py:77
  50.5 5.0 %all-to-all-done.3 = bf16[4,2,8192]{2,1,0:T(2,128)(2,1)S(1)} async-done(((bf16[4,2,8192]{2,1,0:T(2,128)(2,1)}), bf16[4,2,8192]{2,1,0:T(2,128)(2,1)S(1)}, u32[]{:S(2)}, u32[]{:S(2)}) %all-to-all-start.3) | async-done | bytes 131104 | tf_op jit(solution)/shard_map/all_to_all | solution.py:77
  55.5 4.0 %all-to-all-start = ((f32[4,2,2,32,128]{4,3,2,1,0:T(8,128)}), f32[4,2,2,32,128]{4,3,2,1,0:T(8,128)}, u32[]{:S(2)}, u32[]{:S(2)}) async-start(f32[4,2,2,32,128]{4,3,2,1,0:T(8,128)} %broadcast_select_fusion.1), calls=%async_computation | async-start | bytes 524288 | tf_op jit(solution)/shard_map/all_to_all | solution.py:54
  61.8 1.0 %fusion.16 = f32[2,32,128,4]{2,3,1,0:T(4,128)S(1)} fusion(f32[32,2,32,128]{3,2,0,1:T(8,128)S(1)} %pad_maximum_fusion.1, s32[32]{0:T(128)S(1)} %bitcast.179), kind=kOutput, calls=%fused_computation.19 | convolution fusion | flops 12583040 | bytes 1179776 | tf_op jit(solution)/shard_map/lr,radp->adlp/dot_general | solution.py:31
  62.8 3.6 %all-to-all-done = f32[4,2,2,32,128]{4,3,2,1,0:T(8,128)} async-done(((f32[4,2,2,32,128]{4,3,2,1,0:T(8,128)}), f32[4,2,2,32,128]{4,3,2,1,0:T(8,128)}, u32[]{:S(2)}, u32[]{:S(2)}) %all-to-all-start) | async-done | bytes 262176 | tf_op jit(solution)/shard_map/all_to_all | solution.py:54
  66.4 1.2 %copy.72 = f32[4,2,2,32,128]{4,1,0,3,2:T(2,128)S(1)} copy(f32[4,2,2,32,128]{4,3,2,1,0:T(8,128)} %all-to-all-done) | data formatting | bytes 524288 | tf_op jit(solution)/shard_map/all_to_all | solution.py:54
  67.8 1.7 %fusion.13 = f32[2,32,4,128]{3,2,1,0:T(4,128)S(1)} fusion(f32[2,32,128,4]{2,3,1,0:T(4,128)S(1)} %fusion.16, f32[2,32,128,4]{2,3,1,0:T(4,128)S(1)} %fusion.52, f32[56,2,32,128]{3,2,0,1:T(8,128)S(1)} %pad_maximum_fusion, s32[56]{0:T(128)S(1)} %get-tuple-element.5), kind=kOutput, calls=%fused_computation.17 | convolution fusion | flops 22085856 | bytes 2228448 | tf_op jit(solution)/shard_map/lr,radp->adlp/dot_general | solution.py:31
  70.2 10.2 %reduce-scatter.2.cloned.1.call-done = f32[2,32,2,128]{3,1,0,2:T(8,128)} async-done(((f32[2,32,4,128]{3,1,0,2:T(8,128)}), f32[2,32,2,128]{3,1,0,2:T(8,128)}) %reduce-scatter.2.cloned.1.call-update) | async-done | bytes 65552 | tf_op jit(solution)/shard_map/reduce_scatter | solution.py:98
  80.4 1.5 %copy_bitcast_fusion = f32[2,32,256]{2,1,0:T(8,128)} fusion(f32[2,32,2,128]{3,1,0,2:T(8,128)} %reduce-scatter.2.cloned.1.call-done), kind=kLoop, calls=%fused_computation.58 | loop fusion | bytes 131072 | tf_op jit(solution)/shard_map/reshape | solution.py:99
  (64 shorter events, 12.5 us)
Async XLA Ops:
  6.5 54.0 %copy-start = (bf16[1,1,32,2,32,128]{5,4,3,2,1,0:T(8,128)(2,1)S(1)}, bf16[1,1,32,2,32,128]{5,4,3,2,1,0:T(8,128)(2,1)}, u32[]{:S(2)}) copy-start(bf16[1,1,32,2,32,128]{5,4,3,2,1,0:T(8,128)(2,1)} %param.16) | copy-start | bytes 1572868
  8.9 26.8 %all-to-all-start.1 = ((s32[4,1,2]{2,1,0:T(1,128)}), s32[4,1,2]{2,1,0:T(1,128)S(1)}, u32[]{:S(2)}, u32[]{:S(2)}) async-start(s32[4,1,2]{2,1,0:T(1,128)} %bitcast.19), calls=%async_computation.1 | async-start | bytes 4096 | tf_op jit(solution)/shard_map/all_to_all | solution.py:61
  21.7 1.4 %copy-start.4 = (s32[1,1,32]{2,1,0:T(1,128)S(1)}, s32[1,1,32]{2,1,0:T(1,128)}, u32[]{:S(2)}) copy-start(s32[1,1,32]{2,1,0:T(1,128)} %param.14) | copy-start | bytes 388
  21.8 1.9 %copy-start.2 = (bf16[1,1,32,2,32,128]{5,4,3,2,1,0:T(8,128)(2,1)S(1)}, bf16[1,1,32,2,32,128]{5,4,3,2,1,0:T(8,128)(2,1)}, u32[]{:S(2)}) copy-start(bf16[1,1,32,2,32,128]{5,4,3,2,1,0:T(8,128)(2,1)} %param.13) | copy-start | bytes 1572868
  24.8 1.6 %copy-start.1 = (s32[1,1,32]{2,1,0:T(1,128)S(1)}, s32[1,1,32]{2,1,0:T(1,128)}, u32[]{:S(2)}) copy-start(s32[1,1,32]{2,1,0:T(1,128)} %param.15) | copy-start | bytes 388
  35.7 10.6 %all-to-all-start.2 = ((s32[4,1,8]{2,1,0:T(1,128)}), s32[4,1,8]{2,1,0:T(1,128)S(1)}, u32[]{:S(2)}, u32[]{:S(2)}) async-start(s32[4,1,8]{2,1,0:T(1,128)} %bitcast.25), calls=%async_computation.2 | async-start | bytes 4096 | tf_op jit(solution)/shard_map/all_to_all | solution.py:84
  46.3 9.2 %all-to-all-start.3 = ((bf16[4,2,8192]{2,1,0:T(2,128)(2,1)}), bf16[4,2,8192]{2,1,0:T(2,128)(2,1)S(1)}, u32[]{:S(2)}, u32[]{:S(2)}) async-start(bf16[4,2,8192]{2,1,0:T(2,128)(2,1)} %reshape.635), calls=%async_computation.3 | async-start | bytes 262144 | tf_op jit(solution)/shard_map/all_to_all | solution.py:77
  55.5 10.9 %all-to-all-start = ((f32[4,2,2,32,128]{4,3,2,1,0:T(8,128)}), f32[4,2,2,32,128]{4,3,2,1,0:T(8,128)}, u32[]{:S(2)}, u32[]{:S(2)}) async-start(f32[4,2,2,32,128]{4,3,2,1,0:T(8,128)} %broadcast_select_fusion.1), calls=%async_computation | async-start | bytes 524288 | tf_op jit(solution)/shard_map/all_to_all | solution.py:54
  59.6 20.9 %reduce-scatter.2.cloned.1.call-start = ((), (), s32[]{:S(2)}) async-start(), calls=%async_computation.5 | async-start | bytes 196608 | tf_op jit(solution)/shard_map/reduce_scatter | solution.py:98
  61.1 0.7 copy-start.3
Sparse Core Ops, SparseCore 0:
  70.3 10.0 reduce-scatter.1
where the time goes:
time: 89.4 us; the launch traced here: 88.7 us
  waiting for transfers between devices  23 us (26%)
  starting transfers between devices  18.8 us (21%)
  between operations  13.7 us (15%)
  local copies, waits for them, and re-layouts  13.1 us (15%)
  other arithmetic  12.2 us (14%)
  matrix products  7.98 us (9%)
    reduce_scatter x1, waiting for transfers between devices, body(): lax.psum_scatter(cluster_total, 'tgt', scatter_dimension=2, tiled=True)  10.2 us
    all_to_all x1, starting transfers between devices, body(): lax.all_to_all(labels.reshape(owners, CAP), 'src', split_axis=0, concat_a...  6.32 us
    all_to_all x1, starting transfers between devices, body(): lax.all_to_all(slot_far.reshape(owners, slot_depth), 'src', split_axis=0,...  5.09 us
    all_to_all x1, waiting for transfers between devices, body(): lax.all_to_all(outgoing_far.reshape((owners, slot_depth) + coefficients.s...  5.01 us
    dot_general x3, matrix products, complex_apply(): jnp.einsum(pattern, operand, matrices, preferred_element_type=jnp.float32)  4.97 us
    all_to_all x1, waiting for transfers between devices, body(): lax.all_to_all(slot_far.reshape(owners, slot_depth), 'src', split_axis=0,...  4.17 us
    all_to_all x1, starting transfers between devices, body(): lax.all_to_all(outgoing.reshape(owners, CAP, 2, half_dirs, PANEL), 'src',...  4.04 us
    all_to_all x1, waiting for transfers between devices, body(): lax.all_to_all(outgoing.reshape(owners, CAP, 2, half_dirs, PANEL), 'src',...  3.57 us
  transfers between devices with their start and end apart: 5, of which 4 were waited for; matrix products, arithmetic and copies ran while one was open for 28% of the time, Pallas kernels for 0%

commit v1 on v0

v1 whole, which is shorter than its diff:
```python
import functools

import jax
import jax.numpy as jnp
from jax import lax
from jax.experimental import pallas as pl
from jax.experimental.pallas import tpu as pltpu
from jax.sharding import PartitionSpec as P

PANEL = 128
CHUNK = 8
MESH = pl.DeviceIdType.MESH
F32 = jnp.float32
BF16 = jnp.bfloat16
I32 = jnp.int32

PERM, PREV, LAST, SLOT, CLUSTER = range(5)


def shift_of(size):
    assert size & (size - 1) == 0
    return size.bit_length() - 1


def loop(start, stop, step):
    if stop - start <= 8:
        for index in range(start, stop):
            step(index)
    else:

        @pl.loop(start, stop)
        def _(index):
            step(index)


def iota(shape, axis):
    return lax.broadcasted_iota(I32, shape, axis)


def column(row):
    size = row.shape[1]
    eye = iota((size, size), 0) == iota((size, size), 1)
    return jnp.sum(jnp.where(eye, row, 0.0), axis=1, keepdims=True)


def dot_nt(left, right):
    return lax.dot_general(left, right, (((1,), (1,)), ((), ())), preferred_element_type=F32)


def offset_row(owner, me, owners):
    offset = owner - me
    return jnp.where(offset < 0, offset + owners, offset)


def kernel(
    owners, tgts, depth,
    inc_h, nb_h, nsrc, ntgt, fv_h, fsrc, fdst, fu_h, ftgt,
    out_ref,
    inc, nb, fv, fu, stacked, tab, tab_in, tab_s, far_out, far_in, run, near_out, near_in, acc,
    tg_out, tg_in,
    in_sem, nb_sem, tab_sem, lab_send, lab_recv, far_send, far_recv, near_send, near_recv,
    tg_send, tg_recv,
):
    count, half = nb.shape[0], inc.shape[1]
    clusters = inc.shape[2] // PANEL
    far_count, rank = fv.shape[0], fv.shape[2]
    width = depth * rank
    share = clusters // tgts
    me, mine = lax.axis_index("src"), lax.axis_index("tgt")

    def read(step, row, lane, top):
        return jnp.clip(tab_s[step, row, lane], 0, top)

    def owner_at(step):
        return lax.rem(me + step, owners)

    def tgt_at(step):
        return lax.rem(mine + step, tgts)

    barrier = pltpu.get_barrier_semaphore()

    def greet_owner(step):
        pl.semaphore_signal(barrier, inc=1, device_id={"src": owner_at(step)}, device_id_type=MESH)

    def greet_tgt(step):
        pl.semaphore_signal(barrier, inc=1, device_id={"tgt": tgt_at(step)}, device_id_type=MESH)

    loop(1, owners, greet_owner)
    loop(1, tgts, greet_tgt)

    load_inc = pltpu.make_async_copy(inc_h.at[...], inc, in_sem.at[0])
    load_fv = pltpu.make_async_copy(fv_h.at[0, 0], fv, in_sem.at[1])
    load_fu = pltpu.make_async_copy(fu_h.at[0, 0], fu, in_sem.at[2])
    load_inc.start()
    load_fv.start()

    def load_nb(chunk):
        part = pl.ds(chunk * CHUNK, CHUNK)
        return pltpu.make_async_copy(nb_h.at[0, 0, part], nb.at[part], nb_sem.at[chunk])

    for chunk in range(count // CHUNK):
        load_nb(chunk).start()
    load_fu.start()

    target = ntgt[0]
    own_bits = shift_of(clusters)
    step_row = offset_row(lax.shift_right_logical(target, own_bits), me, owners)
    local_row = target & (clusters - 1)
    bucket_row = jnp.where(step_row == 0, local_row, clusters + step_row - 1).astype(F32)
    bucket_col = column(bucket_row)
    local_col = column(local_row.astype(F32))
    at0, at1 = iota((count, count), 0), iota((count, count), 1)
    before = (bucket_col == bucket_row) & (at0 < at1)
    prev = jnp.max(jnp.where(before, at0.astype(F32), -1.0), axis=0, keepdims=True)
    prev = jnp.where(prev < 0, float(count), prev)
    lanes = iota((count, 128), 1).astype(F32)
    in_bucket = bucket_col == lanes
    last = jnp.max(jnp.where(in_bucket, iota((count, 128), 0).astype(F32), -1.0), axis=0, keepdims=True)
    last = jnp.where(last < 0, float(count), last)
    label = jnp.max(jnp.where(in_bucket, local_col, -1.0), axis=0, keepdims=True)

    route = fdst[0]
    far_bits = shift_of(far_count)
    to_row = offset_row(lax.shift_right_logical(route, far_bits), me, owners).astype(F32)
    to_col = column(to_row)
    slot_col = column((route & (far_count - 1)).astype(F32))
    f0, f1 = iota((far_count, far_count), 0), iota((far_count, far_count), 1)
    earlier = jnp.where((to_col == to_row) & (f1 < f0), 1.0, 0.0)
    place = to_col * float(depth) + jnp.sum(earlier, axis=1, keepdims=True)
    hit = place == iota((far_count, 128), 1).astype(F32)
    perm = jnp.sum(jnp.where(hit, iota((far_count, 128), 0).astype(F32), 0.0), axis=0, keepdims=True)
    slot = jnp.sum(jnp.where(hit, slot_col + 1.0, 0.0), axis=0, keepdims=True) - 1.0

    tab[PERM : PERM + 1, :] = perm.astype(I32)
    tab[PREV : PREV + 1, 0:count] = prev.astype(I32)
    tab[LAST : LAST + 1, :] = last.astype(I32)
    tab[SLOT : SLOT + 1, :] = slot.astype(I32)
    tab[CLUSTER : CLUSTER + 1, :] = label.astype(I32)
    own_tab = pltpu.make_async_copy(tab, tab_s.at[0], tab_sem.at[0])
    own_tab.start()

    pl.semaphore_wait(barrier, owners - 1 + tgts - 1)

    def send_lab(step):
        return pltpu.make_async_remote_copy(
            src_ref=tab, dst_ref=tab_in.at[step], send_sem=lab_send.at[step],
            recv_sem=lab_recv.at[step], device_id={"src": owner_at(step)}, device_id_type=MESH)

    def send_far(step):
        return pltpu.make_async_remote_copy(
            src_ref=far_out.at[step], dst_ref=far_in.at[step], send_sem=far_send.at[step],
            recv_sem=far_recv.at[step], device_id={"src": owner_at(step)}, device_id_type=MESH)

    def send_near(step):
        return pltpu.make_async_remote_copy(
            src_ref=near_out.at[step], dst_ref=near_in.at[step], send_sem=near_send.at[step],
            recv_sem=near_recv.at[step], device_id={"src": owner_at(step)}, device_id_type=MESH)

    def send_tgt(step):
        return pltpu.make_async_remote_copy(
            src_ref=tg_out.at[step], dst_ref=tg_in.at[step], send_sem=tg_send.at[step],
            recv_sem=tg_recv.at[step], device_id={"tgt": tgt_at(step)}, device_id_type=MESH)

    loop(1, owners, lambda step: send_lab(step).start())

    load_inc.wait()
    for c in range(clusters):
        part = slice(c * PANEL, (c + 1) * PANEL)
        re, im = inc[0, :, part], inc[1, :, part]
        stacked[c, 0:half, 0:PANEL] = re
        stacked[c, 0:half, PANEL:] = -im
        stacked[c, half:, 0:PANEL] = im
        stacked[c, half:, PANEL:] = re
    run[count] = jnp.zeros(run.shape[1:], F32)

    own_tab.wait()
    load_fv.wait()
    lane_item = lax.shift_right_logical(iota((1, width), 1), shift_of(rank))

    def far_step(step):
        picks = [read(0, PERM, step * depth + j, far_count - 1) for j in range(depth)]
        factors = jnp.concatenate(
            [jnp.concatenate([fv[f, 0], fv[f, 1]], axis=1) for f in picks], axis=0)
        source = jnp.zeros((1, width), I32)
        for j, f in enumerate(picks):
            source = jnp.where(lane_item == j, fsrc[0, 0, f], source)
        every = dot_nt(stacked[...].reshape(clusters * 2 * half, 2 * PANEL), factors)
        chosen = every[0 : 2 * half]
        for c in range(1, clusters):
            chosen = jnp.where(source == c, every[c * 2 * half : (c + 1) * 2 * half], chosen)
        return chosen.astype(BF16)

    def far_send_step(step):
        far_out[step] = far_step(step)
        send_far(step).start()

    loop(1, owners, far_send_step)
    far_in[0] = far_step(0)

    @pl.loop(0, count // CHUNK)
    def _(chunk):
        load_nb(chunk).wait()
        for j in range(CHUNK):
            b = chunk * CHUNK + j
            block = jnp.concatenate([nb[b, 0], nb[b, 1]], axis=1)
            product = dot_nt(stacked[nsrc[0, 0, b]], block)
            run[b] = run[read(0, PREV, b, count)] + product

    def near_step(step):
        near_out[step] = run[read(0, LAST, clusters + step - 1, count)].astype(BF16)
        send_near(step).start()

    loop(1, owners, near_step)

    def lab_step(step):
        send_lab(step).wait_recv()
        pltpu.make_async_copy(tab_in.at[step], tab_s.at[step], tab_sem.at[step]).start()

    loop(1, owners, lab_step)
    load_fu.wait()

    def far_apply(step):
        slots = [tab_s[step, SLOT, step * depth + j] for j in range(depth)]
        kept = [jnp.clip(s, 0, far_count - 1) for s in slots]
        factors = jnp.concatenate([fu[s, 0] for s in kept] + [fu[s, 1] for s in kept], axis=0)
        into = jnp.full((1, width), -1, I32)
        for j in range(depth):
            into = jnp.where(lane_item == j, jnp.where(slots[j] < 0, -1, ftgt[0, 0, kept[j]]), into)
        coeff = far_in[step]
        both = jnp.concatenate([coeff, jnp.concatenate([-coeff[half:], coeff[:half]], axis=0)], axis=1)
        into = jnp.concatenate([into, into], axis=1)
        masked = jnp.concatenate(
            [both * jnp.where(into == c, 1.0, 0.0).astype(BF16) for c in range(clusters)], axis=0)
        return jnp.dot(masked, factors, preferred_element_type=F32).reshape(acc.shape)

    total = far_apply(0)
    for c in range(clusters):
        acc[c] = total[c] + run[read(0, LAST, c, count)]

    def far_in_step(step):
        pltpu.make_async_copy(tab_in.at[step], tab_s.at[step], tab_sem.at[step]).wait()
        send_far(step).wait_recv()
        acc[...] += far_apply(step)

    loop(1, owners, far_in_step)

    def near_in_step(step):
        send_near(step).wait_recv()
        where_to = tab_s[step, CLUSTER, clusters + step - 1]
        value = near_in[step].astype(F32)
        for c in range(clusters):
            acc[c] += jnp.where(where_to == c, value, 0.0)

    loop(1, owners, near_in_step)

    for step in range(1, tgts):
        tg_out[step] = acc[pl.ds(tgt_at(step) * share, share)].astype(BF16)
        send_tgt(step).start()
    for step in range(1, tgts):
        send_tgt(step).wait_recv()
    for i in range(share):
        value = acc[mine * share + i]
        for step in range(1, tgts):
            value = value + tg_in[step, i].astype(F32)
        part = slice(i * PANEL, (i + 1) * PANEL)
        out_ref[0, :, part] = value[:half]
        out_ref[1, :, part] = value[half:]

    def drain(step):
        send_lab(step).wait_send()
        send_far(step).wait_send()
        send_near(step).wait_send()

    loop(1, owners, drain)
    for step in range(1, tgts):
        send_tgt(step).wait_send()


def body(incident, near_blocks, near_src, near_tgt, far_v, far_src, far_dst, far_u, far_tgt):
    owners, tgts = lax.axis_size("src"), lax.axis_size("tgt")
    half = incident.shape[1]
    clusters = incident.shape[2] // PANEL
    count, far_count, rank = near_blocks.shape[2], far_v.shape[2], far_v.shape[4]
    depth = max(4, far_count // owners)
    share = clusters // tgts
    rows = 2 * half
    hbm = pl.BlockSpec(memory_space=pltpu.HBM)
    vmem = pl.BlockSpec(memory_space=pltpu.VMEM)
    smem = pl.BlockSpec(memory_space=pltpu.SMEM)
    dma = pltpu.SemaphoreType.DMA
    return pl.pallas_call(
        functools.partial(kernel, owners, tgts, depth),
        out_shape=jax.ShapeDtypeStruct((2, half, share * PANEL), F32),
        in_specs=[hbm, hbm, smem, vmem, hbm, smem, vmem, hbm, smem],
        out_specs=vmem,
        scratch_shapes=[
            pltpu.VMEM(incident.shape, BF16),
            pltpu.VMEM(near_blocks.shape[2:], BF16),
            pltpu.VMEM(far_v.shape[2:], BF16),
            pltpu.VMEM(far_u.shape[2:], BF16),
            pltpu.VMEM((clusters, rows, 2 * PANEL), BF16),
            pltpu.VMEM((8, 128), I32),
            pltpu.VMEM((owners, 8, 128), I32),
            pltpu.SMEM((owners, 8, 128), I32),
            pltpu.VMEM((owners, rows, depth * rank), BF16),
            pltpu.VMEM((owners, rows, depth * rank), BF16),
            pltpu.VMEM((count + 1, rows, PANEL), F32),
            pltpu.VMEM((owners, rows, PANEL), BF16),
            pltpu.VMEM((owners, rows, PANEL), BF16),
            pltpu.VMEM((clusters, rows, PANEL), F32),
            pltpu.VMEM((tgts, share, rows, PANEL), BF16),
            pltpu.VMEM((tgts, share, rows, PANEL), BF16),
            dma((3,)),
            dma((count // CHUNK,)),
            dma((owners,)),
            dma((owners,)), dma((owners,)),
            dma((owners,)), dma((owners,)),
            dma((owners,)), dma((owners,)),
            dma((tgts,)), dma((tgts,)),
        ],
        compiler_params=pltpu.CompilerParams(
            collective_id=0, has_side_effects=True, vmem_limit_bytes=40 * 1024 * 1024),
    )(incident, near_blocks, near_src, near_tgt, far_v, far_src, far_dst, far_u, far_tgt)


def solution(mesh):
    grid = ("groups", "src")
    blocks = P(grid, "tgt", None, None, None, None)
    index = P(grid, "tgt", None)
    return jax.shard_map(
        body,
        mesh=mesh,
        in_specs=(P(None, "dir", grid), blocks, index, index, blocks, index, index, blocks, index),
        out_specs=P(None, "dir", ("groups", "src", "tgt")),
        check_vma=False,
    )
```

time: 89.4 us -> 24.8 us (0.28)
  waiting for transfers between devices: 23 us -> 0 us
  starting transfers between devices: 18.8 us -> 0 us
  Pallas kernels: 0 us -> 15.6 us
  between operations: 13.7 us -> 0.02 us
  other arithmetic: 12.2 us -> 0 us
  matrix products: 7.98 us -> 0 us
  local copies, waits for them, and re-layouts: 13.1 us -> 8.86 us
    all_to_all x4 -> x0, starting transfers between devices: 18.8 us -> none  [the longest x1 6.32 us: body(): lax.all_to_all(labels.reshape(owners, CAP), 'src', split_axis=0, concat_a...]
    pallas_call x0 -> x1, Pallas kernels: none -> 15.6 us  [body(): pl.pallas_call(functools.partial(kernel, owners, tgts, depth), out_shape=...]
    all_to_all x4 -> x0, waiting for transfers between devices: 12.8 us -> none  [the longest x1 5.01 us: body(): lax.all_to_all(outgoing_far.reshape((owners, slot_depth) + coefficients.s...]
    reduce_scatter x1 -> x0, waiting for transfers between devices: 10.2 us -> none  [body(): lax.psum_scatter(cluster_total, 'tgt', scatter_dimension=2, tiled=True)]
    dot_general x6 -> x0, matrix products: 7.98 us -> none  [the longest x3 4.97 us: complex_apply(): jnp.einsum(pattern, operand, matrices, preferred_element_type=jnp.float32)]
    unnamed x12 -> x19, local copies, waits for them, and re-layouts: 1.94 us -> 8.86 us
    gather x8 -> x0, local copies, waits for them, and re-layouts: 5.35 us -> none  [the longest x1 1.26 us: body(): partial_value[chosen]]
    select_n x14 -> x0, other arithmetic: 3.87 us -> none  [the longest x1 1.74 us: body(): jnp.where(filled[:, None, None, None], partial_value[chosen], 0.0)]
  transfers between devices with their start and end apart: 5 -> 0, of which waited for: 4 -> 0; matrix products, arithmetic and copies ran while one was open for 28% -> 0% of each run, Pallas kernels for 0% -> 0%
where the time goes in v1:
time: 24.8 us; the launch traced here: 24.4 us
  Pallas kernels  15.6 us (63%)
  local copies, waits for them, and re-layouts  8.86 us (36%)
    pallas_call x1, Pallas kernels, body(): pl.pallas_call(functools.partial(kernel, owners, tgts, depth), out_shape=...  15.6 us
    unnamed x19, local copies, waits for them, and re-layouts  8.86 us

profile of v1, /device:TPU:0, one launch (start us, length us, event | category | flops | bytes accessed | tf_op | source)
XLA Modules:
  0.0 24.4 jit_solution(5425573361879552290)
XLA Ops:
  0.0 0.0 copy-start
  0.0 2.0 %copy-done = bf16[1,1,56,2,128,128]{5,4,3,2,1,0:T(8,128)(2,1)S(1)} copy-done((bf16[1,1,56,2,128,128]{5,4,3,2,1,0:T(8,128)(2,1)S(1)}, bf16[1,1,56,2,128,128]{5,4,3,2,1,0:T(8,128)(2,1)}, u32[]{:S(2)}) %copy-start) | copy-done | bytes 3670040
  2.0 0.0 copy-start.1
  2.0 1.0 %copy-done.1 = bf16[1,1,32,2,32,128]{5,4,3,2,1,0:T(8,128)(2,1)S(1)} copy-done((bf16[1,1,32,2,32,128]{5,4,3,2,1,0:T(8,128)(2,1)S(1)}, bf16[1,1,32,2,32,128]{5,4,3,2,1,0:T(8,128)(2,1)}, u32[]{:S(2)}) %copy-start.1) | copy-done | bytes 524312
  3.1 0.0 copy-start.2
  3.1 1.0 %copy-done.2 = bf16[1,1,32,2,32,128]{5,4,3,2,1,0:T(8,128)(2,1)S(1)} copy-done((bf16[1,1,32,2,32,128]{5,4,3,2,1,0:T(8,128)(2,1)S(1)}, bf16[1,1,32,2,32,128]{5,4,3,2,1,0:T(8,128)(2,1)}, u32[]{:S(2)}) %copy-start.2) | copy-done | bytes 524312
  4.1 0.0 copy-start.3
  4.1 0.8 %copy-done.3 = bf16[2,32,512]{2,1,0:T(8,128)(2,1)S(1)} copy-done((bf16[2,32,512]{2,1,0:T(8,128)(2,1)S(1)}, bf16[2,32,512]{2,1,0:T(8,128)(2,1)}, u32[]{:S(2)}) %copy-start.3) | copy-done | bytes 65560
  5.0 0.0 copy-start.4
  5.0 0.7 %copy-done.4 = s32[1,1,56]{2,1,0:T(1,128)S(1)} copy-done((s32[1,1,56]{2,1,0:T(1,128)S(1)}, s32[1,1,56]{2,1,0:T(1,128)}, u32[]{:S(2)}) %copy-start.4) | copy-done | bytes 248
  5.6 0.0 copy-start.5
  5.6 0.7 %copy-done.5 = s32[1,1,56]{2,1,0:T(1,128)S(1)} copy-done((s32[1,1,56]{2,1,0:T(1,128)S(1)}, s32[1,1,56]{2,1,0:T(1,128)}, u32[]{:S(2)}) %copy-start.5) | copy-done | bytes 248
  6.3 0.0 copy-start.6
  6.3 0.7 %copy-done.6 = s32[1,1,32]{2,1,0:T(1,128)S(1)} copy-done((s32[1,1,32]{2,1,0:T(1,128)S(1)}, s32[1,1,32]{2,1,0:T(1,128)}, u32[]{:S(2)}) %copy-start.6) | copy-done | bytes 152
  6.9 0.0 copy-start.7
  6.9 0.7 %copy-done.7 = s32[1,1,32]{2,1,0:T(1,128)S(1)} copy-done((s32[1,1,32]{2,1,0:T(1,128)S(1)}, s32[1,1,32]{2,1,0:T(1,128)}, u32[]{:S(2)}) %copy-start.7) | copy-done | bytes 152
  7.6 0.0 copy-start.8
  7.6 0.7 %copy-done.8 = s32[1,1,32]{2,1,0:T(1,128)S(1)} copy-done((s32[1,1,32]{2,1,0:T(1,128)S(1)}, s32[1,1,32]{2,1,0:T(1,128)}, u32[]{:S(2)}) %copy-start.8) | copy-done | bytes 152
  8.2 15.6 %shard_map.91 = f32[2,32,256]{2,1,0:T(8,128)S(1)} custom-call(bf16[2,32,512]{2,1,0:T(8,128)(2,1)S(1)} %copy-done.3, bf16[1,1,56,2,128,128]{5,4,3,2,1,0:T(8,128)(2,1)S(1)} %copy-done, s32[1,1,56]{2,1,0:T(1,128)S(1)} %copy-done.4, s32[1,1,56]{2,1,0:T(1,128)S(1)} %copy-done.5, bf16[1,1,32,2,32,128]{5,4,3,2,1,0:T(8,128)(2,1)S(1)} %copy-done.1, ...), custom_call_target="tpu_custom_call" | custom-call | tf_op jit(solution)/shard_map/pallas_call | solution.py:291
  23.8 0.6 %copy.11 = f32[2,32,256]{2,1,0:T(8,128)} copy(f32[2,32,256]{2,1,0:T(8,128)S(1)} %shard_map.91) | data formatting | bytes 131072
Async XLA Ops:
  0.0 2.0 %copy-start = (bf16[1,1,56,2,128,128]{5,4,3,2,1,0:T(8,128)(2,1)S(1)}, bf16[1,1,56,2,128,128]{5,4,3,2,1,0:T(8,128)(2,1)}, u32[]{:S(2)}) copy-start(bf16[1,1,56,2,128,128]{5,4,3,2,1,0:T(8,128)(2,1)} %nb_h.1) | copy-start | bytes 11010052
  2.0 1.0 %copy-start.1 = (bf16[1,1,32,2,32,128]{5,4,3,2,1,0:T(8,128)(2,1)S(1)}, bf16[1,1,32,2,32,128]{5,4,3,2,1,0:T(8,128)(2,1)}, u32[]{:S(2)}) copy-start(bf16[1,1,32,2,32,128]{5,4,3,2,1,0:T(8,128)(2,1)} %fv_h.1) | copy-start | bytes 1572868
  3.1 1.0 %copy-start.2 = (bf16[1,1,32,2,32,128]{5,4,3,2,1,0:T(8,128)(2,1)S(1)}, bf16[1,1,32,2,32,128]{5,4,3,2,1,0:T(8,128)(2,1)}, u32[]{:S(2)}) copy-start(bf16[1,1,32,2,32,128]{5,4,3,2,1,0:T(8,128)(2,1)} %fu_h.1) | copy-start | bytes 1572868
  4.1 0.8 %copy-start.3 = (bf16[2,32,512]{2,1,0:T(8,128)(2,1)S(1)}, bf16[2,32,512]{2,1,0:T(8,128)(2,1)}, u32[]{:S(2)}) copy-start(bf16[2,32,512]{2,1,0:T(8,128)(2,1)} %inc_h.1) | copy-start | bytes 196612
  5.0 0.7 %copy-start.4 = (s32[1,1,56]{2,1,0:T(1,128)S(1)}, s32[1,1,56]{2,1,0:T(1,128)}, u32[]{:S(2)}) copy-start(s32[1,1,56]{2,1,0:T(1,128)} %nsrc.1) | copy-start | bytes 676
  5.6 0.7 %copy-start.5 = (s32[1,1,56]{2,1,0:T(1,128)S(1)}, s32[1,1,56]{2,1,0:T(1,128)}, u32[]{:S(2)}) copy-start(s32[1,1,56]{2,1,0:T(1,128)} %ntgt.1) | copy-start | bytes 676
  6.3 0.7 %copy-start.6 = (s32[1,1,32]{2,1,0:T(1,128)S(1)}, s32[1,1,32]{2,1,0:T(1,128)}, u32[]{:S(2)}) copy-start(s32[1,1,32]{2,1,0:T(1,128)} %fsrc.1) | copy-start | bytes 388
  6.9 0.7 %copy-start.7 = (s32[1,1,32]{2,1,0:T(1,128)S(1)}, s32[1,1,32]{2,1,0:T(1,128)}, u32[]{:S(2)}) copy-start(s32[1,1,32]{2,1,0:T(1,128)} %fdst.1) | copy-start | bytes 388
  7.6 0.7 %copy-start.8 = (s32[1,1,32]{2,1,0:T(1,128)S(1)}, s32[1,1,32]{2,1,0:T(1,128)}, u32[]{:S(2)}) copy-start(s32[1,1,32]{2,1,0:T(1,128)} %ftgt.1) | copy-start | bytes 388

commit v2 on v1

--- a/solution.py
+++ b/solution.py
@@ -54,9 +54,9 @@
 
 def kernel(
     owners, tgts, depth,
-    inc_h, nb_h, nsrc, ntgt, fv_h, fsrc, fdst, fu_h, ftgt,
+    inc_h, nb_h, nsrc_h, ntgt_h, fv_h, fsrc_h, fdst_h, fu_h, ftgt_h,
     out_ref,
-    inc, nb, fv, fu, stacked, tab, tab_in, tab_s, far_out, far_in, run, near_out, near_in, acc,
+    inc, nb, fv, fu, ntgt, fdst, nsrc, fsrc, ftgt, stacked, tab, tab_in, tab_s, far_out, far_in, run, near_out, near_in, acc,
     tg_out, tg_in,
     in_sem, nb_sem, tab_sem, lab_send, lab_recv, far_send, far_recv, near_send, near_recv,
     tg_send, tg_recv,
@@ -91,8 +91,18 @@
     load_inc = pltpu.make_async_copy(inc_h.at[...], inc, in_sem.at[0])
     load_fv = pltpu.make_async_copy(fv_h.at[0, 0], fv, in_sem.at[1])
     load_fu = pltpu.make_async_copy(fu_h.at[0, 0], fu, in_sem.at[2])
+    load_ntgt = pltpu.make_async_copy(ntgt_h.at[...], ntgt, in_sem.at[3])
+    load_fdst = pltpu.make_async_copy(fdst_h.at[...], fdst, in_sem.at[4])
+    load_fsrc = pltpu.make_async_copy(fsrc_h.at[...], fsrc, in_sem.at[5])
+    load_nsrc = pltpu.make_async_copy(nsrc_h.at[...], nsrc, in_sem.at[6])
+    load_ftgt = pltpu.make_async_copy(ftgt_h.at[...], ftgt, in_sem.at[7])
+    load_ntgt.start()
+    load_fdst.start()
+    load_fsrc.start()
     load_inc.start()
     load_fv.start()
+    load_nsrc.start()
+    load_ftgt.start()
 
     def load_nb(chunk):
         part = pl.ds(chunk * CHUNK, CHUNK)
@@ -102,6 +112,8 @@
         load_nb(chunk).start()
     load_fu.start()
 
+    load_ntgt.wait()
+    load_fdst.wait()
     target = ntgt[0]
     own_bits = shift_of(clusters)
     step_row = offset_row(lax.shift_right_logical(target, own_bits), me, owners)
@@ -174,6 +186,7 @@
     run[count] = jnp.zeros(run.shape[1:], F32)
 
     own_tab.wait()
+    load_fsrc.wait()
     load_fv.wait()
     lane_item = lax.shift_right_logical(iota((1, width), 1), shift_of(rank))
 
@@ -197,6 +210,8 @@
     loop(1, owners, far_send_step)
     far_in[0] = far_step(0)
 
+    load_nsrc.wait()
+
     @pl.loop(0, count // CHUNK)
     def _(chunk):
         load_nb(chunk).wait()
@@ -218,6 +233,7 @@
 
     loop(1, owners, lab_step)
     load_fu.wait()
+    load_ftgt.wait()
 
     def far_apply(step):
         slots = [tab_s[step, SLOT, step * depth + j] for j in range(depth)]
@@ -286,18 +302,22 @@
     rows = 2 * half
     hbm = pl.BlockSpec(memory_space=pltpu.HBM)
     vmem = pl.BlockSpec(memory_space=pltpu.VMEM)
-    smem = pl.BlockSpec(memory_space=pltpu.SMEM)
     dma = pltpu.SemaphoreType.DMA
     return pl.pallas_call(
         functools.partial(kernel, owners, tgts, depth),
         out_shape=jax.ShapeDtypeStruct((2, half, share * PANEL), F32),
-        in_specs=[hbm, hbm, smem, vmem, hbm, smem, vmem, hbm, smem],
+        in_specs=[hbm] * 9,
         out_specs=vmem,
         scratch_shapes=[
             pltpu.VMEM(incident.shape, BF16),
             pltpu.VMEM(near_blocks.shape[2:], BF16),
             pltpu.VMEM(far_v.shape[2:], BF16),
             pltpu.VMEM(far_u.shape[2:], BF16),
+            pltpu.VMEM(near_tgt.shape, I32),
+            pltpu.VMEM(far_dst.shape, I32),
+            pltpu.SMEM(near_src.shape, I32),
+            pltpu.SMEM(far_src.shape, I32),
+            pltpu.SMEM(far_tgt.shape, I32),
             pltpu.VMEM((clusters, rows, 2 * PANEL), BF16),
             pltpu.VMEM((8, 128), I32),
             pltpu.VMEM((owners, 8, 128), I32),
@@ -310,7 +330,7 @@
             pltpu.VMEM((clusters, rows, PANEL), F32),
             pltpu.VMEM((tgts, share, rows, PANEL), BF16),
             pltpu.VMEM((tgts, share, rows, PANEL), BF16),
-            dma((3,)),
+            dma((8,)),
             dma((count // CHUNK,)),
             dma((owners,)),
             dma((owners,)), dma((owners,)),
@@ -319,7 +339,7 @@
             dma((tgts,)), dma((tgts,)),
         ],
         compiler_params=pltpu.CompilerParams(
-            collective_id=0, has_side_effects=True, vmem_limit_bytes=40 * 1024 * 1024),
+            collective_id=0, has_side_effects=True, vmem_limit_bytes=64 * 1024 * 1024),
     )(incident, near_blocks, near_src, near_tgt, far_v, far_src, far_dst, far_u, far_tgt)
 
 

time: 24.8 us -> 17.7 us (0.71)
  local copies, waits for them, and re-layouts: 8.86 us -> 1.47 us
  Pallas kernels: 15.6 us -> 16 us
    unnamed x19 -> x1, local copies, waits for them, and re-layouts: 8.86 us -> 1.47 us
    pallas_call x1, Pallas kernels: 15.6 us -> 16 us  [body(): pl.pallas_call(functools.partial(kernel, owners, tgts, depth), out_shape=...]
where the time goes in v2:
time: 17.7 us; the launch traced here: 17.5 us
  Pallas kernels  16 us (90%)
  local copies, waits for them, and re-layouts  1.47 us (8%)
    pallas_call x1, Pallas kernels, body(): pl.pallas_call(functools.partial(kernel, owners, tgts, depth), out_shape=...  16 us
    unnamed x1, local copies, waits for them, and re-layouts  1.47 us

profile of v2, /device:TPU:0, one launch (start us, length us, event | category | flops | bytes accessed | tf_op | source)
XLA Modules:
  0.0 17.5 jit_solution(3814718164387442485)
XLA Ops:
  0.0 16.0 %shard_map.91 = f32[2,32,256]{2,1,0:T(8,128)} custom-call(bf16[2,32,512]{2,1,0:T(8,128)(2,1)} %inc_h.1, bf16[1,1,56,2,128,128]{5,4,3,2,1,0:T(8,128)(2,1)} %nb_h.1, s32[1,1,56]{2,1,0:T(1,128)} %nsrc_h.1, s32[1,1,56]{2,1,0:T(1,128)} %ntgt_h.1, bf16[1,1,32,2,32,128]{5,4,3,2,1,0:T(8,128)(2,1)} %fv_h.1, s32[1,1,32]{2,1,0:T(1,128)} %fsrc_h.1, s32[1,1,32]{2,1,0:T(1,128)} %fdst_h.1, ...), custom_call_target="tpu_custom_call" | custom-call | tf_op jit(solution)/shard_map/pallas_call | solution.py:306
  16.0 1.5 %copy.11 = f32[2,32,256]{2,1,0:T(8,128)} copy(f32[2,32,256]{2,1,0:T(8,128)} %shard_map.91) | data formatting | bytes 131072

commit v3 on v2

--- a/solution.py
+++ b/solution.py
@@ -305,7 +305,7 @@
     dma = pltpu.SemaphoreType.DMA
     return pl.pallas_call(
         functools.partial(kernel, owners, tgts, depth),
-        out_shape=jax.ShapeDtypeStruct((2, half, share * PANEL), F32),
+        out_shape=pltpu.VMEM((2, half, share * PANEL), F32),
         in_specs=[hbm] * 9,
         out_specs=vmem,
         scratch_shapes=[
@@ -339,7 +339,7 @@
             dma((tgts,)), dma((tgts,)),
         ],
         compiler_params=pltpu.CompilerParams(
-            collective_id=0, has_side_effects=True, vmem_limit_bytes=64 * 1024 * 1024),
+            collective_id=0, has_side_effects=True, vmem_limit_bytes=64 * 1024 * 1024 - 131072),
     )(incident, near_blocks, near_src, near_tgt, far_v, far_src, far_dst, far_u, far_tgt)
 
 

time: 17.7 us -> 16.2 us (0.915)
  local copies, waits for them, and re-layouts: 1.47 us -> 0.63 us
  Pallas kernels: 16 us -> 15.4 us
    unnamed x1, local copies, waits for them, and re-layouts: 1.47 us -> 0.63 us
    pallas_call x1, Pallas kernels: 16 us -> 15.4 us  [body(): pl.pallas_call(functools.partial(kernel, owners, tgts, depth), out_shape=...]
where the time goes in v3:
time: 16.2 us; the launch traced here: 16 us
  Pallas kernels  15.4 us (95%)
  local copies, waits for them, and re-layouts  0.63 us (4%)
    pallas_call x1, Pallas kernels, body(): pl.pallas_call(functools.partial(kernel, owners, tgts, depth), out_shape=...  15.4 us
    unnamed x1, local copies, waits for them, and re-layouts  0.63 us

profile of v3, /device:TPU:0, one launch (start us, length us, event | category | flops | bytes accessed | tf_op | source)
XLA Modules:
  0.0 16.0 jit_solution(12519393582598787408)
XLA Ops:
  0.0 15.4 %shard_map.91 = f32[2,32,256]{2,1,0:T(8,128)S(1)} custom-call(bf16[2,32,512]{2,1,0:T(8,128)(2,1)} %inc_h.1, bf16[1,1,56,2,128,128]{5,4,3,2,1,0:T(8,128)(2,1)} %nb_h.1, s32[1,1,56]{2,1,0:T(1,128)} %nsrc_h.1, s32[1,1,56]{2,1,0:T(1,128)} %ntgt_h.1, bf16[1,1,32,2,32,128]{5,4,3,2,1,0:T(8,128)(2,1)} %fv_h.1, s32[1,1,32]{2,1,0:T(1,128)} %fsrc_h.1, ...), custom_call_target="tpu_custom_call" | custom-call | tf_op jit(solution)/shard_map/pallas_call | solution.py:306
  15.4 0.6 %copy.11 = f32[2,32,256]{2,1,0:T(8,128)} copy(f32[2,32,256]{2,1,0:T(8,128)S(1)} %shard_map.91) | data formatting | bytes 131072

commit v4 on v3

--- a/solution.py
+++ b/solution.py
@@ -56,7 +56,7 @@
     owners, tgts, depth,
     inc_h, nb_h, nsrc_h, ntgt_h, fv_h, fsrc_h, fdst_h, fu_h, ftgt_h,
     out_ref,
-    inc, nb, fv, fu, ntgt, fdst, nsrc, fsrc, ftgt, stacked, tab, tab_in, tab_s, far_out, far_in, run, near_out, near_in, acc,
+    inc, nb, fv, fu, ntgt, fdst, nsrc, fsrc, ftgt, stacked, tab, tab_in, tab_s, far_out, far_in, run, near_out, near_in, acc, acc_near,
     tg_out, tg_in,
     in_sem, nb_sem, tab_sem, lab_send, lab_recv, far_send, far_recv, near_send, near_recv,
     tg_send, tg_recv,
@@ -69,7 +69,7 @@
     me, mine = lax.axis_index("src"), lax.axis_index("tgt")
 
     def read(step, row, lane, top):
-        return jnp.clip(tab_s[step, row, lane], 0, top)
+        return jnp.clip(tab_s[step, 0, row, lane], 0, top)
 
     def owner_at(step):
         return lax.rem(me + step, owners)
@@ -80,7 +80,10 @@
     barrier = pltpu.get_barrier_semaphore()
 
     def greet_owner(step):
-        pl.semaphore_signal(barrier, inc=1, device_id={"src": owner_at(step)}, device_id_type=MESH)
+        for q in range(tgts):
+            pl.semaphore_signal(
+                barrier, inc=1, device_id={"src": owner_at(step), "tgt": tgt_at(q)},
+                device_id_type=MESH)
 
     def greet_tgt(step):
         pl.semaphore_signal(barrier, inc=1, device_id={"tgt": tgt_at(step)}, device_id_type=MESH)
@@ -148,32 +151,38 @@
     tab[LAST : LAST + 1, :] = last.astype(I32)
     tab[SLOT : SLOT + 1, :] = slot.astype(I32)
     tab[CLUSTER : CLUSTER + 1, :] = label.astype(I32)
-    own_tab = pltpu.make_async_copy(tab, tab_s.at[0], tab_sem.at[0])
+    own_tab = pltpu.make_async_copy(tab, tab_s.at[0, 0], tab_sem.at[0, 0])
     own_tab.start()
 
-    pl.semaphore_wait(barrier, owners - 1 + tgts - 1)
-
-    def send_lab(step):
+    pl.semaphore_wait(barrier, owners * tgts - 1)
+
+    def send_lab(step, q):
         return pltpu.make_async_remote_copy(
-            src_ref=tab, dst_ref=tab_in.at[step], send_sem=lab_send.at[step],
-            recv_sem=lab_recv.at[step], device_id={"src": owner_at(step)}, device_id_type=MESH)
+            src_ref=tab, dst_ref=tab_in.at[step, q], send_sem=lab_send.at[step, q],
+            recv_sem=lab_recv.at[step, q],
+            device_id={"src": owner_at(step), "tgt": tgt_at(q)}, device_id_type=MESH)
 
     def send_far(step):
         return pltpu.make_async_remote_copy(
             src_ref=far_out.at[step], dst_ref=far_in.at[step], send_sem=far_send.at[step],
             recv_sem=far_recv.at[step], device_id={"src": owner_at(step)}, device_id_type=MESH)
 
-    def send_near(step):
+    def send_near(step, q):
         return pltpu.make_async_remote_copy(
-            src_ref=near_out.at[step], dst_ref=near_in.at[step], send_sem=near_send.at[step],
-            recv_sem=near_recv.at[step], device_id={"src": owner_at(step)}, device_id_type=MESH)
+            src_ref=near_out.at[step], dst_ref=near_in.at[step, q], send_sem=near_send.at[step, q],
+            recv_sem=near_recv.at[step, q],
+            device_id={"src": owner_at(step), "tgt": tgt_at(q)}, device_id_type=MESH)
 
     def send_tgt(step):
         return pltpu.make_async_remote_copy(
             src_ref=tg_out.at[step], dst_ref=tg_in.at[step], send_sem=tg_send.at[step],
             recv_sem=tg_recv.at[step], device_id={"tgt": tgt_at(step)}, device_id_type=MESH)
 
-    loop(1, owners, lambda step: send_lab(step).start())
+    def lab_start(step):
+        for q in range(tgts):
+            send_lab(step, q).start()
+
+    loop(1, owners, lab_start)
 
     load_inc.wait()
     for c in range(clusters):
@@ -223,20 +232,25 @@
 
     def near_step(step):
         near_out[step] = run[read(0, LAST, clusters + step - 1, count)].astype(BF16)
-        send_near(step).start()
+        for q in range(tgts):
+            send_near(step, q).start()
 
     loop(1, owners, near_step)
 
+    def load_lab(step, q):
+        return pltpu.make_async_copy(tab_in.at[step, q], tab_s.at[step, q], tab_sem.at[step, q])
+
     def lab_step(step):
-        send_lab(step).wait_recv()
-        pltpu.make_async_copy(tab_in.at[step], tab_s.at[step], tab_sem.at[step]).start()
+        for q in range(tgts):
+            send_lab(step, q).wait_recv()
+            load_lab(step, q).start()
 
     loop(1, owners, lab_step)
     load_fu.wait()
     load_ftgt.wait()
 
     def far_apply(step):
-        slots = [tab_s[step, SLOT, step * depth + j] for j in range(depth)]
+        slots = [tab_s[step, 0, SLOT, step * depth + j] for j in range(depth)]
         kept = [jnp.clip(s, 0, far_count - 1) for s in slots]
         factors = jnp.concatenate([fu[s, 0] for s in kept] + [fu[s, 1] for s in kept], axis=0)
         into = jnp.full((1, width), -1, I32)
@@ -254,28 +268,33 @@
         acc[c] = total[c] + run[read(0, LAST, c, count)]
 
     def far_in_step(step):
-        pltpu.make_async_copy(tab_in.at[step], tab_s.at[step], tab_sem.at[step]).wait()
+        for q in range(tgts):
+            load_lab(step, q).wait()
         send_far(step).wait_recv()
         acc[...] += far_apply(step)
 
     loop(1, owners, far_in_step)
-
-    def near_in_step(step):
-        send_near(step).wait_recv()
-        where_to = tab_s[step, CLUSTER, clusters + step - 1]
-        value = near_in[step].astype(F32)
-        for c in range(clusters):
-            acc[c] += jnp.where(where_to == c, value, 0.0)
-
-    loop(1, owners, near_in_step)
 
     for step in range(1, tgts):
         tg_out[step] = acc[pl.ds(tgt_at(step) * share, share)].astype(BF16)
         send_tgt(step).start()
+
+    def near_in_step(step):
+        for q in range(tgts):
+            send_near(step, q).wait_recv()
+            where_to = tab_s[step, q, CLUSTER, clusters + step - 1] - mine * share
+            value = near_in[step, q].astype(F32)
+            for i in range(share):
+                acc_near[i] += jnp.where(where_to == i, value, 0.0)
+
+    for i in range(share):
+        acc_near[i] = acc[mine * share + i]
+    loop(1, owners, near_in_step)
+
     for step in range(1, tgts):
         send_tgt(step).wait_recv()
     for i in range(share):
-        value = acc[mine * share + i]
+        value = acc_near[i]
         for step in range(1, tgts):
             value = value + tg_in[step, i].astype(F32)
         part = slice(i * PANEL, (i + 1) * PANEL)
@@ -283,9 +302,10 @@
         out_ref[1, :, part] = value[half:]
 
     def drain(step):
-        send_lab(step).wait_send()
         send_far(step).wait_send()
-        send_near(step).wait_send()
+        for q in range(tgts):
+            send_lab(step, q).wait_send()
+            send_near(step, q).wait_send()
 
     loop(1, owners, drain)
     for step in range(1, tgts):
@@ -320,22 +340,23 @@
             pltpu.SMEM(far_tgt.shape, I32),
             pltpu.VMEM((clusters, rows, 2 * PANEL), BF16),
             pltpu.VMEM((8, 128), I32),
-            pltpu.VMEM((owners, 8, 128), I32),
-            pltpu.SMEM((owners, 8, 128), I32),
+            pltpu.VMEM((owners, tgts, 8, 128), I32),
+            pltpu.SMEM((owners, tgts, 8, 128), I32),
             pltpu.VMEM((owners, rows, depth * rank), BF16),
             pltpu.VMEM((owners, rows, depth * rank), BF16),
             pltpu.VMEM((count + 1, rows, PANEL), F32),
             pltpu.VMEM((owners, rows, PANEL), BF16),
-            pltpu.VMEM((owners, rows, PANEL), BF16),
+            pltpu.VMEM((owners, tgts, rows, PANEL), BF16),
             pltpu.VMEM((clusters, rows, PANEL), F32),
+            pltpu.VMEM((share, rows, PANEL), F32),
             pltpu.VMEM((tgts, share, rows, PANEL), BF16),
             pltpu.VMEM((tgts, share, rows, PANEL), BF16),
             dma((8,)),
             dma((count // CHUNK,)),
-            dma((owners,)),
+            dma((owners, tgts)),
+            dma((owners, tgts)), dma((owners, tgts)),
             dma((owners,)), dma((owners,)),
-            dma((owners,)), dma((owners,)),
-            dma((owners,)), dma((owners,)),
+            dma((owners, tgts)), dma((owners, tgts)),
             dma((tgts,)), dma((tgts,)),
         ],
         compiler_params=pltpu.CompilerParams(

time: 16.2 us -> 15.1 us (0.932)
  Pallas kernels: 15.4 us -> 14.3 us
    pallas_call x1, Pallas kernels: 15.4 us -> 14.3 us  [body(): pl.pallas_call(functools.partial(kernel, owners, tgts, depth), out_shape=...]
where the time goes in v4:
time: 15.1 us; the launch traced here: 15 us
  Pallas kernels  14.3 us (95%)
  local copies, waits for them, and re-layouts  0.63 us (4%)
    pallas_call x1, Pallas kernels, body(): pl.pallas_call(functools.partial(kernel, owners, tgts, depth), out_shape=...  14.3 us
    unnamed x1, local copies, waits for them, and re-layouts  0.63 us

profile of v4, /device:TPU:0, one launch (start us, length us, event | category | flops | bytes accessed | tf_op | source)
XLA Modules:
  0.0 15.0 jit_solution(13953428614741512635)
XLA Ops:
  0.0 14.3 %shard_map.91 = f32[2,32,256]{2,1,0:T(8,128)S(1)} custom-call(bf16[2,32,512]{2,1,0:T(8,128)(2,1)} %inc_h.1, bf16[1,1,56,2,128,128]{5,4,3,2,1,0:T(8,128)(2,1)} %nb_h.1, s32[1,1,56]{2,1,0:T(1,128)} %nsrc_h.1, s32[1,1,56]{2,1,0:T(1,128)} %ntgt_h.1, bf16[1,1,32,2,32,128]{5,4,3,2,1,0:T(8,128)(2,1)} %fv_h.1, s32[1,1,32]{2,1,0:T(1,128)} %fsrc_h.1, ...), custom_call_target="tpu_custom_call" | custom-call | tf_op jit(solution)/shard_map/pallas_call | solution.py:326
  14.3 0.6 %copy.11 = f32[2,32,256]{2,1,0:T(8,128)} copy(f32[2,32,256]{2,1,0:T(8,128)S(1)} %shard_map.91) | data formatting | bytes 131072

commit v5 on v4

--- a/solution.py
+++ b/solution.py
@@ -179,7 +179,10 @@
             recv_sem=tg_recv.at[step], device_id={"tgt": tgt_at(step)}, device_id_type=MESH)
 
     def lab_start(step):
-        for q in range(tgts):
+        send_lab(step, 0).start()
+
+    def near_lab_start(step):
+        for q in range(1, tgts):
             send_lab(step, q).start()
 
     loop(1, owners, lab_start)
@@ -217,6 +220,7 @@
         send_far(step).start()
 
     loop(1, owners, far_send_step)
+    loop(1, owners, near_lab_start)
     far_in[0] = far_step(0)
 
     load_nsrc.wait()
@@ -232,7 +236,7 @@
 
     def near_step(step):
         near_out[step] = run[read(0, LAST, clusters + step - 1, count)].astype(BF16)
-        for q in range(tgts):
+        for q in reversed(range(tgts)):
             send_near(step, q).start()
 
     loop(1, owners, near_step)
@@ -241,9 +245,8 @@
         return pltpu.make_async_copy(tab_in.at[step, q], tab_s.at[step, q], tab_sem.at[step, q])
 
     def lab_step(step):
-        for q in range(tgts):
-            send_lab(step, q).wait_recv()
-            load_lab(step, q).start()
+        send_lab(step, 0).wait_recv()
+        load_lab(step, 0).start()
 
     loop(1, owners, lab_step)
     load_fu.wait()
@@ -268,8 +271,7 @@
         acc[c] = total[c] + run[read(0, LAST, c, count)]
 
     def far_in_step(step):
-        for q in range(tgts):
-            load_lab(step, q).wait()
+        load_lab(step, 0).wait()
         send_far(step).wait_recv()
         acc[...] += far_apply(step)
 
@@ -279,8 +281,17 @@
         tg_out[step] = acc[pl.ds(tgt_at(step) * share, share)].astype(BF16)
         send_tgt(step).start()
 
+    def near_lab_step(step):
+        for q in range(1, tgts):
+            send_lab(step, q).wait_recv()
+            load_lab(step, q).start()
+
+    loop(1, owners, near_lab_step)
+
     def near_in_step(step):
         for q in range(tgts):
+            if q:
+                load_lab(step, q).wait()
             send_near(step, q).wait_recv()
             where_to = tab_s[step, q, CLUSTER, clusters + step - 1] - mine * share
             value = near_in[step, q].astype(F32)

time: 15.1 us -> 15 us (level)
  no operation moved by 1% of the time
where the time goes in v5:
time: 15 us; the launch traced here: 14.9 us
  Pallas kernels  14.2 us (95%)
  local copies, waits for them, and re-layouts  0.63 us (4%)
    pallas_call x1, Pallas kernels, body(): pl.pallas_call(functools.partial(kernel, owners, tgts, depth), out_shape=...  14.2 us
    unnamed x1, local copies, waits for them, and re-layouts  0.63 us

profile of v5, /device:TPU:0, one launch (start us, length us, event | category | flops | bytes accessed | tf_op | source)
XLA Modules:
  0.0 14.9 jit_solution(297235783434276139)
XLA Ops:
  0.0 14.2 %shard_map.91 = f32[2,32,256]{2,1,0:T(8,128)S(1)} custom-call(bf16[2,32,512]{2,1,0:T(8,128)(2,1)} %inc_h.1, bf16[1,1,56,2,128,128]{5,4,3,2,1,0:T(8,128)(2,1)} %nb_h.1, s32[1,1,56]{2,1,0:T(1,128)} %nsrc_h.1, s32[1,1,56]{2,1,0:T(1,128)} %ntgt_h.1, bf16[1,1,32,2,32,128]{5,4,3,2,1,0:T(8,128)(2,1)} %fv_h.1, s32[1,1,32]{2,1,0:T(1,128)} %fsrc_h.1, ...), custom_call_target="tpu_custom_call" | custom-call | tf_op jit(solution)/shard_map/pallas_call | solution.py:337
  14.3 0.6 %copy.11 = f32[2,32,256]{2,1,0:T(8,128)} copy(f32[2,32,256]{2,1,0:T(8,128)S(1)} %shard_map.91) | data formatting | bytes 131072
